TPU v7x, 32 devices: a whole 2x2x4 slice. The times are simulated.
32 devices in a mesh: stn: 8 (over y, x, core), tm: 4 (over z).
Axes of the slice: x: 2, y: 2, z: 4, core: 2. Of those that a mesh axis runs over, the one named last changes fastest.
Arguments:
- samples: bfloat16 [512, 524288], P('stn', 'tm'), may hold values from -6 to 6
Outputs:
- visibilities: float32 [32, 2, 512, 512], P(('stn', 'tm'))
All inputs are finite; a program needn't handle non-finite values.
Results may differ from a plain program's by a relative error of at most 0.0062.
Values may be sent and summed in bfloat16 or wider, within the bound.
No kernel may reach another device: no remote copies, remote signals or barrier semaphores. Data moves between devices by JAX's collectives and lax.ppermute only.
A program may use at most 256 MiB of HBM per device.

v0:
```python
import jax
import jax.numpy as jnp
from jax import lax
from jax.sharding import PartitionSpec as P

FRAME = 8192
TAPS = 12
CH_DEV = 1


def passed_along(array, axis, by):
    peers = lax.axis_size(axis)
    pairs = [(i, i + by) for i in range(peers) if 0 <= i + by < peers]
    return lax.ppermute(array, axis, pairs)


def prototype():
    length = TAPS * FRAME
    place = jnp.arange(length, dtype=jnp.int32).astype(jnp.float32)
    centred = (place - 0.5 * length + 0.5) / FRAME
    window = 0.54 - 0.46 * jnp.cos(2.0 * jnp.pi * place / (length - 1))
    return (jnp.sinc(centred) * window).reshape(TAPS, FRAME)


def transform_table(kept_channels, first_channel):
    sample_index = jnp.arange(FRAME, dtype=jnp.int32)
    column = jnp.arange(2 * kept_channels, dtype=jnp.int32)
    channel = first_channel + column // 2
    phase = channel[:, None] * sample_index[None, :] % FRAME
    angle = 2.0 * jnp.pi / FRAME * phase.astype(jnp.float32)
    scaling = (2.0 / FRAME) ** 0.5
    table = jnp.where((column % 2 == 0)[:, None], jnp.cos(angle), -jnp.sin(angle)) * scaling
    return table.astype(jnp.bfloat16)


def filter_frames(padded, prototype_taps, out_frames):
    margin_frames = TAPS - 1
    frame_major = jnp.swapaxes(padded, 0, 1)
    running = jnp.zeros((out_frames, padded.shape[0], FRAME), jnp.float32)
    for tap_index in range(TAPS):
        begin = margin_frames - tap_index
        running = running + prototype_taps[tap_index] * frame_major[
            begin : begin + out_frames
        ].astype(jnp.float32)
    return running


def project_spectra(transform, filtered):
    return lax.dot_general(
        transform, filtered, (((1,), (2,)), ((), ())), preferred_element_type=jnp.float32
    )


def on_device(samples):
    station_inputs, sample_count = samples.shape
    frame_count = sample_count // FRAME
    margin_frames = TAPS - 1
    stations = lax.axis_size("stn")
    time_blocks = lax.axis_size("tm")
    kept_channels = CH_DEV * stations * time_blocks
    first_channel = FRAME // 4 - kept_channels // 2
    prototype_taps = prototype()
    transform = transform_table(kept_channels, first_channel)
    blocks = samples.reshape(station_inputs, frame_count, FRAME)
    tail_samples = samples[:, sample_count - margin_frames * FRAME :]
    arrived = passed_along(tail_samples, "tm", 1)
    padded = jnp.concatenate(
        [arrived.reshape(station_inputs, margin_frames, FRAME), blocks], axis=1
    )
    running = filter_frames(padded, prototype_taps, frame_count)
    combined = project_spectra(transform, running.astype(jnp.bfloat16))
    rounded = combined.astype(jnp.bfloat16).reshape(2 * kept_channels, frame_count * station_inputs)
    turned = lax.all_to_all(
        rounded.reshape(2 * kept_channels, 1, frame_count * station_inputs),
        ("stn", "tm"),
        split_axis=0,
        concat_axis=1,
        tiled=True,
    )
    arranged = turned.reshape(CH_DEV, 2, stations, time_blocks, frame_count, station_inputs)
    swapped = jnp.stack([arranged[:, 1], -arranged[:, 0]], axis=1)
    real_part = jnp.einsum(
        "crstfi,crutfj->csiuj", arranged, arranged, preferred_element_type=jnp.float32
    )
    imag_part = jnp.einsum(
        "crstfi,crutfj->csiuj", swapped, arranged, preferred_element_type=jnp.float32
    )
    all_inputs = stations * station_inputs
    real_part = real_part.reshape(CH_DEV, all_inputs, all_inputs)
    imag_part = imag_part.reshape(CH_DEV, all_inputs, all_inputs)
    return jnp.stack([real_part, imag_part], axis=1) * (1.0 / (time_blocks * frame_count))


def solution(mesh):
    placed = (P("stn", "tm"),)
    return jax.shard_map(
        on_device,
        mesh=mesh,
        in_specs=placed,
        out_specs=P(("stn", "tm"), None, None, None),
        check_vma=False,
    )
```

profile of v0, /device:TPU:0, one launch (start us, length us, event | category | flops | bytes accessed | tf_op | source)
XLA Modules:
  0.0 383.2 jit_solution(2052932514378693440)
XLA Ops:
  0.0 0.0 copy-start
  0.0 6.2 %slice.94 = bf16[64,90112]{1,0:T(8,128)(2,1)S(1)} slice(bf16[64,131072]{1,0:T(8,128)(2,1)} %param.1), slice={[0:64], [40960:131072]} | slice | bytes 23068672 | tf_op jit(solution)/shard_map/slice | solution.py:65
  6.2 5.9 %collective-permute-start = (bf16[64,90112]{1,0:T(8,128)(2,1)S(1)}, bf16[64,90112]{1,0:T(8,128)(2,1)S(1)}, u32[]{:S(2)}, u32[]{:S(2)}) collective-permute-start(bf16[64,90112]{1,0:T(8,128)(2,1)S(1)} %slice.94), channel_id=1, source_target_pairs={{0,1},{1,2},{2,3},{4,5},{5,6},{6,7},{8,9},{9,10},{10,11},{12,13},{... | collective-permute-start | bytes 34603016 | tf_op jit(solution)/shard_map/ppermute | solution.py:14
  12.2 0.0 copy-done
  12.2 6.7 %copy.26 = bf16[8,16,8,8192]{3,2,0,1:T(8,128)(2,1)} copy(bf16[8,16,8,8192]{3,2,1,0:T(8,128)(2,1)S(1)} %bitcast.55) | data formatting | bytes 33554432 | tf_op jit(solution)/shard_map/reshape | solution.py:64
  18.8 1.8 fusion.21
  20.7 237.9 %collective-permute-done = bf16[64,90112]{1,0:T(8,128)(2,1)S(1)} collective-permute-done((bf16[64,90112]{1,0:T(8,128)(2,1)S(1)}, bf16[64,90112]{1,0:T(8,128)(2,1)S(1)}, u32[]{:S(2)}, u32[]{:S(2)}) %collective-permute-start) | collective-permute-done | bytes 11534368 | tf_op jit(solution)/shard_map/ppermute | solution.py:14
  258.5 4.9 %copy.27 = bf16[8,11,8,8192]{3,2,0,1:T(8,128)(2,1)} copy(bf16[8,11,8,8192]{3,2,1,0:T(8,128)(2,1)S(1)} %bitcast.57) | data formatting | bytes 23068672 | tf_op jit(solution)/shard_map/reshape | solution.py:68
  263.4 19.6 %maximum_bitcast_fusion = bf16[27,64,8192]{2,1,0:T(8,128)(2,1)} fusion(bf16[64,16,8192]{2,0,1:T(8,128)(2,1)} %bitcast.54, bf16[64,11,8192]{2,0,1:T(8,128)(2,1)} %bitcast.56), kind=kLoop, calls=%fused_computation.1 | loop fusion | flops 14155776 | bytes 56623104 | tf_op jit(solution)/shard_map/transpose | solution.py:38
  283.0 78.6 %fusion.7 = bf16[64,16,64]{2,0,1:T(8,128)(2,1)S(1)} fusion(bf16[27,64,8192]{2,1,0:T(8,128)(2,1)} %maximum_bitcast_fusion, f32[8192]{0:T(1024)S(1)} %get-tuple-element.6, f32[8192]{0:T(1024)S(1)} %get-tuple-element.7, f32[8192]{0:T(1024)S(1)} %get-tuple-element.8, f32[8192]{0:T(1024)S(1)} %get-tuple-element.9, f32[8192]{0:T(1024)S(1)} %get-tuple-element.10, ...), kind=kOutput, calls=%fused_computation.18 | convolution fusion | flops 1385234432 | bytes 201851200 | tf_op jit(solution)/shard_map/dot_general | solution.py:49
  361.6 0.2 copy.13
  361.8 0.2 reshape_reshape.4
  361.9 0.5 broadcast.100
  362.4 1.4 reduce.1
  363.8 0.1 reshape.150
  363.9 15.0 %all_to_all.15 = bf16[32,2,1024]{2,1,0:T(2,128)(2,1)S(1)} all-to-all(bf16[32,2,1024]{2,1,0:T(2,128)(2,1)S(1)} %reshape.150), channel_id=1, replica_groups=mesh['stn'=8,'tm'=4] {'stn','tm'}, dimensions={0} | all-to-all | bytes 262144 | tf_op jit(solution)/shard_map/all_to_all | solution.py:73
  378.8 0.1 reshape.151
  378.9 0.7 reduce
  379.7 0.1 all_to_all.12
  379.8 0.2 reshape.143
  380.0 0.2 reshape.141
  380.2 0.1 maximum_bitcast_fusion.1
  380.2 0.2 copy.18
  380.4 0.2 reshape.145
  380.6 0.2 copy.16
  380.8 0.2 reshape.142
  381.0 0.3 convolution_bitcast_fusion.1
  381.4 0.3 convolution_bitcast_fusion
  381.7 1.6 maximum_multiply_fusion
  (5 shorter events, 0.1 us)
Async XLA Ops:
  0.0 12.2 %copy-start = (bf16[64,131072]{1,0:T(8,128)(2,1)S(1)}, bf16[64,131072]{1,0:T(8,128)(2,1)}, u32[]{:S(2)}) copy-start(bf16[64,131072]{1,0:T(8,128)(2,1)} %param.1) | copy-start | bytes 50331652
  6.2 252.3 %collective-permute-start = (bf16[64,90112]{1,0:T(8,128)(2,1)S(1)}, bf16[64,90112]{1,0:T(8,128)(2,1)S(1)}, u32[]{:S(2)}, u32[]{:S(2)}) collective-permute-start(bf16[64,90112]{1,0:T(8,128)(2,1)S(1)} %slice.94), channel_id=1, source_target_pairs={{0,1},{1,2},{2,3},{4,5},{5,6},{6,7},{8,9},{9,10},{10,11},{12,13},{... | collective-permute-start | bytes 34603016 | tf_op jit(solution)/shard_map/ppermute | solution.py:14
where the time goes:
time: 383 us
  waiting for transfers between devices  238 us (62%)
  matrix products  79.2 us (21%)
  other arithmetic  25.1 us (7%)
  local copies, waits for them, and re-layouts  20 us (5%)
  blocking collectives  15 us (4%)
  starting transfers between devices  5.93 us (2%)
    ppermute x1, waiting for transfers between devices, passed_along(): return lax.ppermute(array, axis, pairs)  238 us
    dot_general x1, matrix products, project_spectra(): lax.dot_general(transform, filtered, (((1,), (2,)), ((), ())), preferred_...  78.6 us
    transpose x1, other arithmetic, filter_frames(): frame_major = jnp.swapaxes(padded, 0, 1)  19.6 us
    all_to_all x1, blocking collectives, on_device(): lax.all_to_all(rounded.reshape(2 * kept_channels, 1, frame_count * statio...  15 us
  transfers between devices with their start and end apart: 1, of which 1 were waited for; matrix products, arithmetic and copies ran while one was open for 2% of the time, Pallas kernels for 0%

commit v1 on v0

v1 whole, which is shorter than its diff:
```python
import functools

import jax
import jax.numpy as jnp
import ml_dtypes
import numpy as np
from jax import lax
from jax.experimental import pallas as pl
from jax.experimental.pallas import tpu as pltpu
from jax.sharding import PartitionSpec as P

FRAME = 8192
TAPS = 12
CH_DEV = 1
LANES = 128
SUBLANES = 8
GROUP = 4
DEPTH = 1024


def tables(kept):
    half = kept // 2
    lane = np.arange(FRAME // 2)
    block, inside = lane // LANES, lane % LANES
    even = 2 * LANES * block + np.where(inside % 2 == 0, inside, LANES + inside - 1)
    odd = 2 * LANES * block + np.where(inside % 2 == 0, inside + 1, LANES + inside)
    length = TAPS * FRAME
    place = np.arange(length, dtype=np.float64)
    window = 0.54 - 0.46 * np.cos(2.0 * np.pi * place / (length - 1))
    prototype = (np.sinc((place - 0.5 * length + 0.5) / FRAME) * window).reshape(TAPS, FRAME)
    turned, middle, taps = [], [], []
    for order in (even, odd):
        sign = 1.0 - 2.0 * (order // 2 % 2)
        phase = np.arange(1, half + 1)[:, None] * order[None, :] % FRAME
        angle = 2.0 * np.pi / FRAME * phase
        rows = np.concatenate([np.cos(angle), -np.sin(angle)]) * sign
        turned.append(rows * (2.0 / FRAME) ** 0.5)
        middle.append(np.broadcast_to(sign * (2.0 / FRAME) ** 0.5, (SUBLANES, FRAME // 2)))
        taps.append(np.concatenate([prototype[:, order], np.zeros((2 * SUBLANES - TAPS, FRAME // 2))]))
    rounded = np.concatenate([np.stack(turned), np.stack(middle)], axis=1).astype(ml_dtypes.bfloat16)
    return rounded.astype(np.float32), np.stack(taps).astype(np.float32)


def spectra_kernel(kept, frames, inputs, samples, turned, taps, out, held, turned_v, taps_v, weights, parted, sums,
                   middle, plus, minus, centre, sem, table_sem):
    half = kept // 2
    groups = frames // GROUP
    width = GROUP * FRAME
    columns = GROUP * inputs
    tiles = columns // LANES
    half_rows = frames * inputs // LANES
    copies = [
        pltpu.make_async_copy(samples.at[:, pl.ds(g * width, width)], held.at[g], sem.at[g]) for g in range(groups)
    ]
    table_copies = [
        pltpu.make_async_copy(turned, turned_v, table_sem.at[0]),
        pltpu.make_async_copy(taps, taps_v, table_sem.at[1]),
    ]
    for copy in table_copies:
        copy.start()
    for copy in copies:
        copy.start()
    for ref in (sums, middle, plus, minus, centre):
        ref[...] = jnp.zeros_like(ref)
    for copy in table_copies:
        copy.wait()

    for parity in range(2):

        def weigh(step, carry):
            at = pl.ds(pl.multiple_of(step * 512, 512), 512)
            rows = turned_v[parity, :kept, at]
            for k in range(TAPS):
                weights[parity, k * kept : (k + 1) * kept, at] = (rows * taps_v[parity, k : k + 1, at]).astype(
                    jnp.bfloat16
                )
            weights[parity, TAPS * kept :, at] = (
                turned_v[parity, kept : kept + 1, at] * taps_v[parity, :, at]
            ).astype(jnp.bfloat16)
            return carry

        lax.fori_loop(0, FRAME // 2 // 512, weigh, 0)

    even_lane = lax.broadcasted_iota(jnp.int32, (inputs, LANES), 1) % 2 == 0
    sublane = lax.broadcasted_iota(jnp.int32, (SUBLANES, LANES), 0)

    def group_step(g, carry):
        pltpu.make_async_copy(samples.at[:, pl.ds(0, width)], held.at[g], sem.at[g]).wait()
        totals = [None, None]
        for begin in range(0, FRAME // 2, DEPTH):
            for f in range(GROUP):
                for at in range(begin, begin + DEPTH, LANES):
                    left = held[g, :, f * FRAME + 2 * at : f * FRAME + 2 * at + LANES]
                    right = held[g, :, f * FRAME + 2 * at + LANES : f * FRAME + 2 * at + 2 * LANES]
                    rows = slice(f * inputs, (f + 1) * inputs)
                    parted[0, rows, at : at + LANES] = jnp.where(even_lane, left, pltpu.roll(right, 1, 1))
                    parted[1, rows, at : at + LANES] = jnp.where(even_lane, pltpu.roll(left, LANES - 1, 1), right)
            for parity in range(2):
                product = lax.dot_general(
                    weights[parity, :, begin : begin + DEPTH],
                    parted[parity, :, begin : begin + DEPTH],
                    (((1,), (1,)), ((), ())),
                    preferred_element_type=jnp.float32,
                )
                totals[parity] = product if totals[parity] is None else totals[parity] + product
        for parity in range(2):
            total = totals[parity]
            for k in range(TAPS):
                for tile in range(tiles):
                    lanes = slice(tile * LANES, (tile + 1) * LANES)
                    to = g * tiles + k // 2 + tile
                    sums[parity, k % 2, to] += total[k * kept : (k + 1) * kept, lanes]
                    slab = total[TAPS * kept + k // SUBLANES * SUBLANES :][:SUBLANES, lanes]
                    middle[parity, k % 2, to] += jnp.where(sublane == k % SUBLANES, slab, 0.0)
        return carry

    lax.fori_loop(0, groups, group_step, 0)

    low = lax.broadcasted_iota(jnp.int32, (1, LANES), 1) < LANES // 2

    def joined(ref, parity, tile):
        later = pltpu.roll(ref[parity, 1, tile], LANES // 2, 1)
        if tile == 0:
            earlier = jnp.zeros_like(later)
        else:
            earlier = pltpu.roll(ref[parity, 1, tile - 1], LANES // 2, 1)
        return ref[parity, 0, tile] + jnp.where(low, earlier, later)

    block = 2 * 2 * half_rows
    for tile in range(sums.shape[2]):
        e = joined(sums, 0, tile)
        o = joined(sums, 1, tile)
        e_re, e_im, o_re, o_im = e[:half], e[half:], o[:half], o[half:]
        real = pl.ds(tile, half, stride=block)
        imag = pl.ds(2 * half_rows + tile, half, stride=block)
        plus[real, :] = e_re + o_im
        plus[imag, :] = e_im - o_re
        minus[real, :] = e_re - o_im
        minus[imag, :] = -e_im - o_re
        centre[tile : tile + 1, :] = jnp.sum(joined(middle, 0, tile), axis=0, keepdims=True)
        centre[2 * half_rows + tile : 2 * half_rows + tile + 1, :] = -jnp.sum(
            joined(middle, 1, tile), axis=0, keepdims=True
        )
    for h in range(1, half + 1):
        rows = slice((h - 1) * block, h * block)
        out[half - h] = minus[rows].astype(jnp.bfloat16)
        if h < half:
            out[half + h] = plus[rows].astype(jnp.bfloat16)
    out[half] = centre[...].astype(jnp.bfloat16)


def block_spectra(samples, kept):
    inputs, count = samples.shape
    frames = count // FRAME
    half = kept // 2
    half_rows = frames * inputs // LANES
    turned, taps = tables(kept)
    rows = TAPS * kept + 2 * SUBLANES
    tiles = (frames + TAPS) * inputs // LANES
    any_spec = pl.BlockSpec(memory_space=pl.ANY)
    return pl.pallas_call(
        functools.partial(spectra_kernel, kept, frames, inputs),
        out_shape=jax.ShapeDtypeStruct((kept, 4 * half_rows, LANES), jnp.bfloat16),
        in_specs=[any_spec] * 3,
        out_specs=pl.BlockSpec(memory_space=pltpu.VMEM),
        scratch_shapes=[
            pltpu.VMEM((frames // GROUP, inputs, GROUP * FRAME), jnp.bfloat16),
            pltpu.VMEM(turned.shape, jnp.float32),
            pltpu.VMEM(taps.shape, jnp.float32),
            pltpu.VMEM((2, rows, FRAME // 2), jnp.bfloat16),
            pltpu.VMEM((2, GROUP * inputs, FRAME // 2), jnp.bfloat16),
            pltpu.VMEM((2, 2, tiles, kept, LANES), jnp.float32),
            pltpu.VMEM((2, 2, tiles, SUBLANES, LANES), jnp.float32),
            pltpu.VMEM((half * 4 * half_rows, LANES), jnp.float32),
            pltpu.VMEM((half * 4 * half_rows, LANES), jnp.float32),
            pltpu.VMEM((4 * half_rows, LANES), jnp.float32),
            pltpu.SemaphoreType.DMA((frames // GROUP,)),
            pltpu.SemaphoreType.DMA((2,)),
        ],
        compiler_params=pltpu.CompilerParams(vmem_limit_bytes=60 << 20),
    )(samples, turned, taps)


def correlate_kernel(stations, time_blocks, half_rows, scaling, arrived, out, spectra):
    inputs = stations * LANES // 2

    @pl.when(pl.program_id(0) == 0)
    def _():
        low = lax.broadcasted_iota(jnp.int32, (1, LANES), 1) < LANES // 2

        def own(station, part):
            rows = []
            for z in range(time_blocks):
                here = arrived[station * time_blocks + z, 2 * half_rows * part : 2 * half_rows * (part + 1)]
                total = here[:half_rows].astype(jnp.float32)
                if z > 0:
                    total += last[half_rows:].astype(jnp.float32)
                last = here
                rows.append(total)
            return jnp.concatenate(rows)

        for pair in range(stations // 2):
            parts = []
            for part in range(2):
                first, second = own(2 * pair, part), own(2 * pair + 1, part)
                parts.append(
                    jnp.concatenate(
                        [
                            jnp.where(low, first, pltpu.roll(second, LANES // 2, 1)),
                            jnp.where(low, pltpu.roll(first, LANES // 2, 1), second),
                        ]
                    )
                )
            lanes = slice(pair * LANES, (pair + 1) * LANES)
            spectra[:, lanes] = jnp.concatenate(parts).astype(jnp.bfloat16)
            spectra[:, inputs + pair * LANES : inputs + (pair + 1) * LANES] = jnp.concatenate(
                [parts[1], -parts[0]]
            ).astype(jnp.bfloat16)

    size = out.shape[2]
    begin = pl.multiple_of(pl.program_id(0) * size, LANES)
    out[0, 0] = scaling * lax.dot_general(
        spectra[:, pl.ds(begin, size)],
        spectra[:, :inputs],
        (((0,), (0,)), ((), ())),
        preferred_element_type=jnp.float32,
    )


def correlate(arrived, stations, time_blocks):
    sources, rows, _ = arrived.shape
    half_rows = rows // 4
    inputs = stations * LANES // 2
    size = min(256, inputs)
    per_part = inputs // size
    frames = time_blocks * half_rows * 2
    return pl.pallas_call(
        functools.partial(correlate_kernel, stations, time_blocks, half_rows, 1.0 / frames),
        out_shape=jax.ShapeDtypeStruct((CH_DEV, 2, inputs, inputs), jnp.float32),
        grid=(2 * per_part,),
        in_specs=[pl.BlockSpec(memory_space=pltpu.VMEM)],
        out_specs=pl.BlockSpec((1, 1, size, inputs), lambda i: (0, i // per_part, i % per_part, 0)),
        scratch_shapes=[pltpu.VMEM((2 * frames, 2 * inputs), jnp.bfloat16)],
        compiler_params=pltpu.CompilerParams(vmem_limit_bytes=32 << 20),
    )(arrived)


def on_device(samples):
    stations = lax.axis_size("stn")
    time_blocks = lax.axis_size("tm")
    kept = CH_DEV * stations * time_blocks
    partial = block_spectra(samples, kept)
    arrived = lax.all_to_all(partial, ("stn", "tm"), split_axis=0, concat_axis=0, tiled=True)
    return correlate(arrived, stations, time_blocks)


def solution(mesh):
    return jax.shard_map(
        on_device,
        mesh=mesh,
        in_specs=(P("stn", "tm"),),
        out_specs=P(("stn", "tm"), None, None, None),
        check_vma=False,
    )
```

time: 383 us -> 35.7 us (0.09)
  waiting for transfers between devices: 238 us -> 0 us
  matrix products: 79.2 us -> 0 us
  other arithmetic: 25.1 us -> 0 us
  local copies, waits for them, and re-layouts: 20 us -> 0 us
  Pallas kernels: 0 us -> 18 us
  starting transfers between devices: 5.93 us -> 0 us
    ppermute x1 -> x0, waiting for transfers between devices: 238 us -> none  [passed_along(): return lax.ppermute(array, axis, pairs)]
    dot_general x3 -> x0, matrix products: 79.2 us -> none  [the longest x1 78.6 us: project_spectra(): lax.dot_general(transform, filtered, (((1,), (2,)), ((), ())), preferred_...]
    transpose x1 -> x0, other arithmetic: 19.6 us -> none  [filter_frames(): frame_major = jnp.swapaxes(padded, 0, 1)]
    pallas_call x0 -> x2, Pallas kernels: none -> 18 us  [the longest x1 15.5 us: block_spectra(): pl.pallas_call(functools.partial(spectra_kernel, kept, frames, inputs), o...]
    reshape x3 -> x0, local copies, waits for them, and re-layouts: 11.7 us -> none  [the longest x1 6.66 us: on_device(): blocks = samples.reshape(station_inputs, frame_count, FRAME)]
    slice x2 -> x0, local copies, waits for them, and re-layouts: 6.25 us -> none  [the longest x1 6.22 us: on_device(): tail_samples = samples[:, sample_count - margin_frames * FRAME:]]
    ppermute x1 -> x0, starting transfers between devices: 5.93 us -> none  [passed_along(): return lax.ppermute(array, axis, pairs)]
  transfers between devices with their start and end apart: 1 -> 0, of which waited for: 1 -> 0; matrix products, arithmetic and copies ran while one was open for 2% -> 0% of each run, Pallas kernels for 0% -> 0%
where the time goes in v1:
time: 35.7 us; the launch traced here: 35.5 us
  Pallas kernels  18 us (50%)
  blocking collectives  17.5 us (49%)
    all_to_all x1, blocking collectives, on_device(): lax.all_to_all(partial, ('stn', 'tm'), split_axis=0, concat_axis=0, tiled...  17.5 us
    pallas_call x1, Pallas kernels, block_spectra(): pl.pallas_call(functools.partial(spectra_kernel, kept, frames, inputs), o...  15.5 us
    pallas_call x1, Pallas kernels, correlate(): pl.pallas_call(functools.partial(correlate_kernel, stations, time_blocks,...  2.5 us

profile of v1, /device:TPU:0, one launch (start us, length us, event | category | flops | bytes accessed | tf_op | source)
XLA Modules:
  0.0 35.5 jit_solution(3218369655627291409)
XLA Ops:
  0.0 15.5 %shard_map.37 = bf16[32,32,128]{2,1,0:T(8,128)(2,1)} custom-call(bf16[64,131072]{1,0:T(8,128)(2,1)} %samples.1, f32[2,40,4096]{2,1,0:T(8,128)} %constant.4.clone.turned, f32[2,16,4096]{2,1,0:T(8,128)} %constant.5.clone.taps), custom_call_target="tpu_custom_call" | custom-call | tf_op jit(solution)/shard_map/pallas_call | solution.py:161
  15.5 17.5 %all_to_all.5.arrived = bf16[32,32,128]{2,1,0:T(8,128)(2,1)S(1)} all-to-all(bf16[32,32,128]{2,1,0:T(8,128)(2,1)} %shard_map.37), channel_id=1, replica_groups=mesh['stn'=8,'tm'=4] {'stn','tm'}, dimensions={0} | all-to-all | bytes 524288 | tf_op jit(solution)/shard_map/all_to_all | solution.py:253
  33.0 2.5 %shard_map.38 = f32[1,2,512,512]{3,2,1,0:T(8,128)} custom-call(bf16[32,32,128]{2,1,0:T(8,128)(2,1)S(1)} %all_to_all.5.arrived), custom_call_target="tpu_custom_call" | custom-call | tf_op jit(solution)/shard_map/pallas_call | solution.py:237

commit v2 on v1

v2 whole, which is shorter than its diff:
```python
import functools

import jax
import jax.numpy as jnp
import ml_dtypes
import numpy as np
from jax import lax
from jax.experimental import pallas as pl
from jax.experimental.pallas import tpu as pltpu
from jax.sharding import PartitionSpec as P

FRAME = 8192
TAPS = 12
CH_DEV = 1
LANES = 128
SUBLANES = 8
GROUP = 4
DEPTH = 1024
AHEAD = 5
GROUPS_AHEAD = 2
CORRELATED = 256
NEAR = 256


def tables(kept):
    half = kept // 2
    lane = np.arange(FRAME // 2)
    block, inside = lane // LANES, lane % LANES
    even = 2 * LANES * block + np.where(inside % 2 == 0, inside, LANES + inside - 1)
    odd = 2 * LANES * block + np.where(inside % 2 == 0, (inside - 1) % LANES, LANES + inside)
    length = TAPS * FRAME
    place = np.arange(length, dtype=np.float64)
    window = 0.54 - 0.46 * np.cos(2.0 * np.pi * place / (length - 1))
    prototype = (np.sinc((place - 0.5 * length + 0.5) / FRAME) * window).reshape(TAPS, FRAME)
    turned, middle, taps = [], [], []
    for order in (even, odd):
        sign = 1.0 - 2.0 * (order // 2 % 2)
        phase = np.arange(1, half + 1)[:, None] * order[None, :] % FRAME
        angle = 2.0 * np.pi / FRAME * phase
        rows = np.concatenate([np.cos(angle), -np.sin(angle)]) * sign
        turned.append(rows * (2.0 / FRAME) ** 0.5)
        middle.append(np.broadcast_to(sign * (2.0 / FRAME) ** 0.5, (SUBLANES, FRAME // 2)))
        taps.append(np.concatenate([prototype[:, order], np.zeros((2 * SUBLANES - TAPS, FRAME // 2))]))
    rounded = np.concatenate([np.stack(turned), np.stack(middle)], axis=1).astype(ml_dtypes.bfloat16)
    return rounded, np.stack(taps).astype(np.float32)


def spectra_kernel(kept, frames, inputs, samples, turned, taps, out, held, turned_v, taps_v, weights, added, sums, middle,
                   plus, minus, centre, piece_sem, frame_sem):
    half = kept // 2
    groups = frames // GROUP
    columns = GROUP * inputs
    tiles = columns // LANES
    half_rows = frames * inputs // LANES
    pieces = FRAME // 2 // DEPTH

    def frame_copy(f):
        at = pl.ds(pl.multiple_of(f * FRAME, FRAME), FRAME)
        return pltpu.make_async_copy(samples.at[:, at], held.at[f], frame_sem.at[f])

    def piece_copies(p):
        table = pl.ds(p * DEPTH, DEPTH)
        lanes = pl.ds(p * 2 * DEPTH, 2 * DEPTH)
        yield pltpu.make_async_copy(turned.at[:, :, table], turned_v.at[:, :, table], piece_sem.at[p, GROUP])
        yield pltpu.make_async_copy(taps.at[:, :, table], taps_v.at[:, :, table], piece_sem.at[p, GROUP + 1])
        for f in range(GROUP):
            yield pltpu.make_async_copy(
                samples.at[:, pl.ds(f * FRAME + p * 2 * DEPTH, 2 * DEPTH)], held.at[f, :, lanes], piece_sem.at[p, f]
            )

    def start_piece(p):
        if p < pieces:
            for copy in piece_copies(p):
                copy.start()
        elif p < pieces + frames - GROUP:
            frame_copy(GROUP + p - pieces).start()

    for p in range(AHEAD):
        start_piece(p)
    for ref in (sums, middle, plus, minus, centre):
        ref[...] = jnp.zeros_like(ref)

    even_lane = lax.broadcasted_iota(jnp.int32, (inputs, LANES), 1) % 2 == 0
    sublane = lax.broadcasted_iota(jnp.int32, (SUBLANES, LANES), 0)

    def weigh(at):
        for parity in range(2):
            rows = turned_v[parity, :kept, at].astype(jnp.float32)
            for k in range(TAPS):
                weights[parity, k * kept : (k + 1) * kept, at] = (rows * taps_v[parity, k : k + 1, at]).astype(
                    jnp.bfloat16
                )
            weights[parity, TAPS * kept :, at] = (
                turned_v[parity, kept : kept + 1, at].astype(jnp.float32) * taps_v[parity, :, at]
            ).astype(jnp.bfloat16)

    def parted(g, near):
        even, odd = [], []
        for f in range(GROUP):
            even_lanes, odd_lanes = [], []
            for at in range(near, near + NEAR, LANES):
                left = held[g * GROUP + f, :, 2 * at : 2 * at + LANES]
                right = held[g * GROUP + f, :, 2 * at + LANES : 2 * at + 2 * LANES]
                moved = pltpu.roll(jnp.where(even_lane, right, left), 1, 1)
                even_lanes.append(jnp.where(even_lane, left, moved))
                odd_lanes.append(jnp.where(even_lane, moved, right))
            even.append(jnp.concatenate(even_lanes, axis=1))
            odd.append(jnp.concatenate(odd_lanes, axis=1))
        return jnp.concatenate(even), jnp.concatenate(odd)

    def group_step(g, first):
        if not first:
            for f in range(GROUP):
                frame_copy(g * GROUP + f).wait()

            @pl.when(g + GROUPS_AHEAD < groups)
            def _():
                for f in range(GROUP):
                    frame_copy((g + GROUPS_AHEAD) * GROUP + f).start()

        for p in range(pieces):
            begin = p * DEPTH
            if first:
                for copy in piece_copies(p):
                    copy.wait()
                start_piece(p + AHEAD)
            totals = [None, None]
            for near in range(begin, begin + DEPTH, NEAR):
                at = slice(near, near + NEAR)
                if first:
                    weigh(at)
                for parity, values in enumerate(parted(g, near)):
                    product = lax.dot_general(
                        weights[parity, :, at], values, (((1,), (1,)), ((), ())), preferred_element_type=jnp.float32
                    )
                    totals[parity] = product if totals[parity] is None else totals[parity] + product
            for parity in range(2):
                if p == 0:
                    added[parity] = totals[parity]
                else:
                    added[parity] += totals[parity]
        if first:
            for p in range(pieces + AHEAD, pieces + GROUP * GROUPS_AHEAD):
                start_piece(p)
        for parity in range(2):
            for k in range(TAPS):
                for tile in range(tiles):
                    lanes = slice(tile * LANES, (tile + 1) * LANES)
                    to = g * tiles + k // 2 + tile
                    sums[parity, k % 2, to] += added[parity, k * kept : (k + 1) * kept, lanes]
                    slab = added[parity, pl.ds(TAPS * kept + k // SUBLANES * SUBLANES, SUBLANES), lanes]
                    middle[parity, k % 2, to] += jnp.where(sublane == k % SUBLANES, slab, 0.0)

    group_step(0, True)

    def later_step(g, carry):
        group_step(g, False)
        return carry

    lax.fori_loop(1, groups, later_step, 0)

    low = lax.broadcasted_iota(jnp.int32, (1, LANES), 1) < LANES // 2

    def joined(ref, parity, tile):
        later = pltpu.roll(ref[parity, 1, tile], LANES // 2, 1)
        if tile == 0:
            earlier = jnp.zeros_like(later)
        else:
            earlier = pltpu.roll(ref[parity, 1, tile - 1], LANES // 2, 1)
        return ref[parity, 0, tile] + jnp.where(low, earlier, later)

    block = 2 * 2 * half_rows
    for tile in range(sums.shape[2]):
        e = joined(sums, 0, tile)
        o = joined(sums, 1, tile)
        e_re, e_im, o_re, o_im = e[:half], e[half:], o[:half], o[half:]
        real = pl.ds(tile, half, stride=block)
        imag = pl.ds(2 * half_rows + tile, half, stride=block)
        plus[real, :] = e_re + o_im
        plus[imag, :] = e_im - o_re
        minus[real, :] = e_re - o_im
        minus[imag, :] = -e_im - o_re
        centre[tile : tile + 1, :] = jnp.sum(joined(middle, 0, tile), axis=0, keepdims=True)
        centre[2 * half_rows + tile : 2 * half_rows + tile + 1, :] = -jnp.sum(
            joined(middle, 1, tile), axis=0, keepdims=True
        )
    for h in range(1, half + 1):
        rows = slice((h - 1) * block, h * block)
        out[half - h] = minus[rows].astype(jnp.bfloat16)
        if h < half:
            out[half + h] = plus[rows].astype(jnp.bfloat16)
    out[half] = centre[...].astype(jnp.bfloat16)


def block_spectra(samples, kept):
    inputs, count = samples.shape
    frames = count // FRAME
    half = kept // 2
    half_rows = frames * inputs // LANES
    turned, taps = tables(kept)
    rows = TAPS * kept + 2 * SUBLANES
    tiles = (frames + TAPS) * inputs // LANES
    any_spec = pl.BlockSpec(memory_space=pl.ANY)
    return pl.pallas_call(
        functools.partial(spectra_kernel, kept, frames, inputs),
        out_shape=jax.ShapeDtypeStruct((kept, 4 * half_rows, LANES), jnp.bfloat16),
        in_specs=[any_spec] * 3,
        out_specs=pl.BlockSpec(memory_space=pltpu.VMEM),
        scratch_shapes=[
            pltpu.VMEM((frames, inputs, FRAME), jnp.bfloat16),
            pltpu.VMEM(turned.shape, jnp.bfloat16),
            pltpu.VMEM(taps.shape, jnp.float32),
            pltpu.VMEM((2, rows, FRAME // 2), jnp.bfloat16),
            pltpu.VMEM((2, rows, GROUP * inputs), jnp.float32),
            pltpu.VMEM((2, 2, tiles, kept, LANES), jnp.float32),
            pltpu.VMEM((2, 2, tiles, SUBLANES, LANES), jnp.float32),
            pltpu.VMEM((half * 4 * half_rows, LANES), jnp.float32),
            pltpu.VMEM((half * 4 * half_rows, LANES), jnp.float32),
            pltpu.VMEM((4 * half_rows, LANES), jnp.float32),
            pltpu.SemaphoreType.DMA((FRAME // 2 // DEPTH, GROUP + 2)),
            pltpu.SemaphoreType.DMA((frames,)),
        ],
        compiler_params=pltpu.CompilerParams(vmem_limit_bytes=60 << 20),
    )(samples, turned, taps)


def correlate_kernel(stations, time_blocks, half_rows, scaling, arrived, out, spectra, held, sem):
    inputs = stations * LANES // 2
    low = lax.broadcasted_iota(jnp.int32, (1, LANES), 1) < LANES // 2

    def own(station, part):
        rows = []
        for z in range(time_blocks):
            here = arrived[station * time_blocks + z, 2 * half_rows * part : 2 * half_rows * (part + 1)]
            total = here[:half_rows].astype(jnp.float32)
            if z > 0:
                total += last[half_rows:].astype(jnp.float32)
            last = here
            rows.append(total)
        return jnp.concatenate(rows)

    for pair in range(stations // 2):
        parts = []
        for part in range(2):
            first, second = own(2 * pair, part), own(2 * pair + 1, part)
            parts.append(
                jnp.concatenate(
                    [
                        jnp.where(low, first, pltpu.roll(second, LANES // 2, 1)),
                        jnp.where(low, pltpu.roll(first, LANES // 2, 1), second),
                    ]
                )
            )
        lanes = slice(pair * LANES, (pair + 1) * LANES)
        spectra[:, lanes] = jnp.concatenate(parts).astype(jnp.bfloat16)
        spectra[:, inputs + pair * LANES : inputs + (pair + 1) * LANES] = jnp.concatenate(
            [parts[1], -parts[0]]
        ).astype(jnp.bfloat16)

    size = min(CORRELATED, inputs)
    copies = []
    for part in range(2):
        for begin in range(0, inputs, size):
            rows = slice(begin, begin + size)
            held[part, rows] = scaling * lax.dot_general(
                spectra[:, part * inputs + begin : part * inputs + begin + size],
                spectra[:, :inputs],
                (((0,), (0,)), ((), ())),
                preferred_element_type=jnp.float32,
            )
            copy = pltpu.make_async_copy(held.at[part, rows], out.at[0, part, rows], sem.at[len(copies)])
            copy.start()
            copies.append(copy)
    for copy in copies:
        copy.wait()


def correlate(arrived, stations, time_blocks):
    sources, rows, _ = arrived.shape
    half_rows = rows // 4
    inputs = stations * LANES // 2
    frames = time_blocks * half_rows * 2
    return pl.pallas_call(
        functools.partial(correlate_kernel, stations, time_blocks, half_rows, 1.0 / frames),
        out_shape=jax.ShapeDtypeStruct((CH_DEV, 2, inputs, inputs), jnp.float32),
        in_specs=[pl.BlockSpec(memory_space=pltpu.VMEM)],
        out_specs=pl.BlockSpec(memory_space=pl.ANY),
        scratch_shapes=[
            pltpu.VMEM((2 * frames, 2 * inputs), jnp.bfloat16),
            pltpu.VMEM((2, inputs, inputs), jnp.float32),
            pltpu.SemaphoreType.DMA((2 * inputs // min(CORRELATED, inputs),)),
        ],
        compiler_params=pltpu.CompilerParams(vmem_limit_bytes=32 << 20),
    )(arrived)


def on_device(samples):
    stations = lax.axis_size("stn")
    time_blocks = lax.axis_size("tm")
    kept = CH_DEV * stations * time_blocks
    partial = block_spectra(samples, kept)
    arrived = lax.all_to_all(partial, ("stn", "tm"), split_axis=0, concat_axis=0, tiled=True)
    return correlate(arrived, stations, time_blocks)


def solution(mesh):
    return jax.shard_map(
        on_device,
        mesh=mesh,
        in_specs=(P("stn", "tm"),),
        out_specs=P(("stn", "tm"), None, None, None),
        check_vma=False,
    )
```

time: 35.7 us -> 31.4 us (0.88)
  Pallas kernels: 18 us -> 13.6 us
    pallas_call x1, Pallas kernels: 15.5 us -> 11.9 us  [block_spectra(): pl.pallas_call(functools.partial(spectra_kernel, kept, frames, inputs), o...]
    pallas_call x1, Pallas kernels: 2.5 us -> 1.7 us  [correlate(): pl.pallas_call(functools.partial(correlate_kernel, stations, time_blocks,...]
where the time goes in v2:
time: 31.4 us; the launch traced here: 31.1 us
  blocking collectives  17.5 us (56%)
  Pallas kernels  13.6 us (43%)
    all_to_all x1, blocking collectives, on_device(): lax.all_to_all(partial, ('stn', 'tm'), split_axis=0, concat_axis=0, tiled...  17.5 us
    pallas_call x1, Pallas kernels, block_spectra(): pl.pallas_call(functools.partial(spectra_kernel, kept, frames, inputs), o...  11.9 us
    pallas_call x1, Pallas kernels, correlate(): pl.pallas_call(functools.partial(correlate_kernel, stations, time_blocks,...  1.7 us

profile of v2, /device:TPU:0, one launch (start us, length us, event | category | flops | bytes accessed | tf_op | source)
XLA Modules:
  0.0 31.1 jit_solution(16354362971194112076)
XLA Ops:
  0.0 11.9 %shard_map.37 = bf16[32,32,128]{2,1,0:T(8,128)(2,1)} custom-call(bf16[64,131072]{1,0:T(8,128)(2,1)} %samples.1, bf16[2,40,4096]{2,1,0:T(8,128)(2,1)} %constant.4.clone.turned, f32[2,16,4096]{2,1,0:T(8,128)} %constant.5.clone.taps), custom_call_target="tpu_custom_call" | custom-call | tf_op jit(solution)/shard_map/pallas_call | solution.py:204
  11.9 17.5 %all_to_all.5.arrived = bf16[32,32,128]{2,1,0:T(8,128)(2,1)S(1)} all-to-all(bf16[32,32,128]{2,1,0:T(8,128)(2,1)} %shard_map.37), channel_id=1, replica_groups=mesh['stn'=8,'tm'=4] {'stn','tm'}, dimensions={0} | all-to-all | bytes 524288 | tf_op jit(solution)/shard_map/all_to_all | solution.py:302
  29.4 1.7 %shard_map.38 = f32[1,2,512,512]{3,2,1,0:T(8,128)} custom-call(bf16[32,32,128]{2,1,0:T(8,128)(2,1)S(1)} %all_to_all.5.arrived), custom_call_target="tpu_custom_call" | custom-call | tf_op jit(solution)/shard_map/pallas_call | solution.py:283

commit v3 on v2

--- a/solution.py
+++ b/solution.py
@@ -32,21 +32,22 @@
     place = np.arange(length, dtype=np.float64)
     window = 0.54 - 0.46 * np.cos(2.0 * np.pi * place / (length - 1))
     prototype = (np.sinc((place - 0.5 * length + 0.5) / FRAME) * window).reshape(TAPS, FRAME)
-    turned, middle, taps = [], [], []
+    stacks = []
     for order in (even, odd):
         sign = 1.0 - 2.0 * (order // 2 % 2)
         phase = np.arange(1, half + 1)[:, None] * order[None, :] % FRAME
         angle = 2.0 * np.pi / FRAME * phase
         rows = np.concatenate([np.cos(angle), -np.sin(angle)]) * sign
-        turned.append(rows * (2.0 / FRAME) ** 0.5)
-        middle.append(np.broadcast_to(sign * (2.0 / FRAME) ** 0.5, (SUBLANES, FRAME // 2)))
-        taps.append(np.concatenate([prototype[:, order], np.zeros((2 * SUBLANES - TAPS, FRAME // 2))]))
-    rounded = np.concatenate([np.stack(turned), np.stack(middle)], axis=1).astype(ml_dtypes.bfloat16)
-    return rounded, np.stack(taps).astype(np.float32)
-
-
-def spectra_kernel(kept, frames, inputs, samples, turned, taps, out, held, turned_v, taps_v, weights, added, sums, middle,
-                   plus, minus, centre, piece_sem, frame_sem):
+        centre = np.broadcast_to(sign, (SUBLANES, FRAME // 2))
+        transform = np.concatenate([rows, centre]) * (2.0 / FRAME) ** 0.5
+        transform = transform.astype(ml_dtypes.bfloat16).astype(np.float32)
+        none = np.zeros((2 * SUBLANES - TAPS, FRAME // 2))
+        stacks.append(np.concatenate([transform, prototype[:, order].astype(np.float32), none]))
+    return np.stack(stacks).astype(np.float32)
+
+
+def spectra_kernel(kept, frames, inputs, samples, table, out, held, table_v, weights, added, sums, middle, plus,
+                   minus, centre, piece_sem, frame_sem):
     half = kept // 2
     groups = frames // GROUP
     columns = GROUP * inputs
@@ -59,10 +60,9 @@
         return pltpu.make_async_copy(samples.at[:, at], held.at[f], frame_sem.at[f])
 
     def piece_copies(p):
-        table = pl.ds(p * DEPTH, DEPTH)
+        at = pl.ds(p * DEPTH, DEPTH)
         lanes = pl.ds(p * 2 * DEPTH, 2 * DEPTH)
-        yield pltpu.make_async_copy(turned.at[:, :, table], turned_v.at[:, :, table], piece_sem.at[p, GROUP])
-        yield pltpu.make_async_copy(taps.at[:, :, table], taps_v.at[:, :, table], piece_sem.at[p, GROUP + 1])
+        yield pltpu.make_async_copy(table.at[:, :, at], table_v.at[:, :, at], piece_sem.at[p, GROUP])
         for f in range(GROUP):
             yield pltpu.make_async_copy(
                 samples.at[:, pl.ds(f * FRAME + p * 2 * DEPTH, 2 * DEPTH)], held.at[f, :, lanes], piece_sem.at[p, f]
@@ -85,14 +85,11 @@
 
     def weigh(at):
         for parity in range(2):
-            rows = turned_v[parity, :kept, at].astype(jnp.float32)
+            rows = table_v[parity, :kept, at]
+            taps = table_v[parity, kept + SUBLANES :, at]
             for k in range(TAPS):
-                weights[parity, k * kept : (k + 1) * kept, at] = (rows * taps_v[parity, k : k + 1, at]).astype(
-                    jnp.bfloat16
-                )
-            weights[parity, TAPS * kept :, at] = (
-                turned_v[parity, kept : kept + 1, at].astype(jnp.float32) * taps_v[parity, :, at]
-            ).astype(jnp.bfloat16)
+                weights[parity, k * kept : (k + 1) * kept, at] = (rows * taps[k : k + 1]).astype(jnp.bfloat16)
+            weights[parity, TAPS * kept :, at] = (table_v[parity, kept : kept + 1, at] * taps).astype(jnp.bfloat16)
 
     def parted(g, near):
         even, odd = [], []
@@ -197,19 +194,18 @@
     frames = count // FRAME
     half = kept // 2
     half_rows = frames * inputs // LANES
-    turned, taps = tables(kept)
+    table = tables(kept)
     rows = TAPS * kept + 2 * SUBLANES
     tiles = (frames + TAPS) * inputs // LANES
     any_spec = pl.BlockSpec(memory_space=pl.ANY)
     return pl.pallas_call(
         functools.partial(spectra_kernel, kept, frames, inputs),
         out_shape=jax.ShapeDtypeStruct((kept, 4 * half_rows, LANES), jnp.bfloat16),
-        in_specs=[any_spec] * 3,
+        in_specs=[any_spec] * 2,
         out_specs=pl.BlockSpec(memory_space=pltpu.VMEM),
         scratch_shapes=[
             pltpu.VMEM((frames, inputs, FRAME), jnp.bfloat16),
-            pltpu.VMEM(turned.shape, jnp.bfloat16),
-            pltpu.VMEM(taps.shape, jnp.float32),
+            pltpu.VMEM(table.shape, jnp.float32),
             pltpu.VMEM((2, rows, FRAME // 2), jnp.bfloat16),
             pltpu.VMEM((2, rows, GROUP * inputs), jnp.float32),
             pltpu.VMEM((2, 2, tiles, kept, LANES), jnp.float32),
@@ -217,11 +213,11 @@
             pltpu.VMEM((half * 4 * half_rows, LANES), jnp.float32),
             pltpu.VMEM((half * 4 * half_rows, LANES), jnp.float32),
             pltpu.VMEM((4 * half_rows, LANES), jnp.float32),
-            pltpu.SemaphoreType.DMA((FRAME // 2 // DEPTH, GROUP + 2)),
+            pltpu.SemaphoreType.DMA((FRAME // 2 // DEPTH, GROUP + 1)),
             pltpu.SemaphoreType.DMA((frames,)),
         ],
-        compiler_params=pltpu.CompilerParams(vmem_limit_bytes=60 << 20),
-    )(samples, turned, taps)
+        compiler_params=pltpu.CompilerParams(vmem_limit_bytes=(52 if rows <= 512 else 63) << 20),
+    )(samples, table)
 
 
 def correlate_kernel(stations, time_blocks, half_rows, scaling, arrived, out, spectra, held, sem):

time: 31.4 us -> 30.4 us (0.968)
  Pallas kernels: 13.6 us -> 13 us
    pallas_call x1, Pallas kernels: 11.9 us -> 11.3 us  [block_spectra(): pl.pallas_call(functools.partial(spectra_kernel, kept, frames, inputs), o...]
where the time goes in v3:
time: 30.4 us; the launch traced here: 30.3 us
  blocking collectives  17.3 us (57%)
  Pallas kernels  13 us (43%)
    all_to_all x1, blocking collectives, on_device(): lax.all_to_all(partial, ('stn', 'tm'), split_axis=0, concat_axis=0, tiled...  17.3 us
    pallas_call x1, Pallas kernels, block_spectra(): pl.pallas_call(functools.partial(spectra_kernel, kept, frames, inputs), o...  11.3 us
    pallas_call x1, Pallas kernels, correlate(): pl.pallas_call(functools.partial(correlate_kernel, stations, time_blocks,...  1.7 us

profile of v3, /device:TPU:0, one launch (start us, length us, event | category | flops | bytes accessed | tf_op | source)
XLA Modules:
  0.0 30.3 jit_solution(6019429876492265264)
XLA Ops:
  0.0 11.3 %shard_map.28 = bf16[32,32,128]{2,1,0:T(8,128)(2,1)S(1)} custom-call(bf16[64,131072]{1,0:T(8,128)(2,1)} %samples.1, f32[2,56,4096]{2,1,0:T(8,128)} %constant.2.clone.table), custom_call_target="tpu_custom_call" | custom-call | tf_op jit(solution)/shard_map/pallas_call | solution.py:201
  11.3 17.3 %all_to_all.5.arrived = bf16[32,32,128]{2,1,0:T(8,128)(2,1)S(1)} all-to-all(bf16[32,32,128]{2,1,0:T(8,128)(2,1)S(1)} %shard_map.28), channel_id=1, replica_groups=mesh['stn'=8,'tm'=4] {'stn','tm'}, dimensions={0} | all-to-all | bytes 524288 | tf_op jit(solution)/shard_map/all_to_all | solution.py:298
  28.6 1.7 %shard_map.29 = f32[1,2,512,512]{3,2,1,0:T(8,128)} custom-call(bf16[32,32,128]{2,1,0:T(8,128)(2,1)S(1)} %all_to_all.5.arrived), custom_call_target="tpu_custom_call" | custom-call | tf_op jit(solution)/shard_map/pallas_call | solution.py:279

commit v4 on v3

--- a/solution.py
+++ b/solution.py
@@ -15,9 +15,9 @@
 LANES = 128
 SUBLANES = 8
 GROUP = 4
-DEPTH = 1024
-AHEAD = 5
-GROUPS_AHEAD = 2
+PIECES = (0, 1024, 2048)
+AHEAD = 8
+BY_PIECE = 1
 CORRELATED = 256
 NEAR = 256
 
@@ -53,30 +53,34 @@
     columns = GROUP * inputs
     tiles = columns // LANES
     half_rows = frames * inputs // LANES
-    pieces = FRAME // 2 // DEPTH
+    edges = PIECES + (FRAME // 2,)
+    pieces = len(PIECES)
 
     def frame_copy(f):
         at = pl.ds(pl.multiple_of(f * FRAME, FRAME), FRAME)
         return pltpu.make_async_copy(samples.at[:, at], held.at[f], frame_sem.at[f])
 
-    def piece_copies(p):
-        at = pl.ds(p * DEPTH, DEPTH)
-        lanes = pl.ds(p * 2 * DEPTH, 2 * DEPTH)
-        yield pltpu.make_async_copy(table.at[:, :, at], table_v.at[:, :, at], piece_sem.at[p, GROUP])
-        for f in range(GROUP):
+    def piece_copies(g, p):
+        begin, size = edges[p], edges[p + 1] - edges[p]
+        lanes = pl.ds(2 * begin, 2 * size)
+        sems = piece_sem.at[g * pieces + p]
+        if g == 0:
+            at = pl.ds(begin, size)
+            yield pltpu.make_async_copy(table.at[:, :, at], table_v.at[:, :, at], sems.at[GROUP])
+        for f in range(g * GROUP, (g + 1) * GROUP):
             yield pltpu.make_async_copy(
-                samples.at[:, pl.ds(f * FRAME + p * 2 * DEPTH, 2 * DEPTH)], held.at[f, :, lanes], piece_sem.at[p, f]
+                samples.at[:, pl.ds(f * FRAME + 2 * begin, 2 * size)], held.at[f, :, lanes], sems.at[f - g * GROUP]
             )
 
-    def start_piece(p):
-        if p < pieces:
-            for copy in piece_copies(p):
+    def start(step):
+        if step < BY_PIECE * pieces:
+            for copy in piece_copies(step // pieces, step % pieces):
                 copy.start()
-        elif p < pieces + frames - GROUP:
-            frame_copy(GROUP + p - pieces).start()
-
-    for p in range(AHEAD):
-        start_piece(p)
+        elif step - BY_PIECE * pieces < frames - BY_PIECE * GROUP:
+            frame_copy(BY_PIECE * GROUP + step - BY_PIECE * pieces).start()
+
+    for step in range(AHEAD):
+        start(step)
     for ref in (sums, middle, plus, minus, centre):
         ref[...] = jnp.zeros_like(ref)
 
@@ -105,24 +109,17 @@
             odd.append(jnp.concatenate(odd_lanes, axis=1))
         return jnp.concatenate(even), jnp.concatenate(odd)
 
-    def group_step(g, first):
-        if not first:
+    def group_step(g, by_piece, first=False):
+        if not by_piece:
             for f in range(GROUP):
                 frame_copy(g * GROUP + f).wait()
-
-            @pl.when(g + GROUPS_AHEAD < groups)
-            def _():
-                for f in range(GROUP):
-                    frame_copy((g + GROUPS_AHEAD) * GROUP + f).start()
-
         for p in range(pieces):
-            begin = p * DEPTH
-            if first:
-                for copy in piece_copies(p):
+            if by_piece:
+                for copy in piece_copies(g, p):
                     copy.wait()
-                start_piece(p + AHEAD)
+                start(g * pieces + p + AHEAD)
             totals = [None, None]
-            for near in range(begin, begin + DEPTH, NEAR):
+            for near in range(edges[p], edges[p + 1], NEAR):
                 at = slice(near, near + NEAR)
                 if first:
                     weigh(at)
@@ -136,9 +133,6 @@
                     added[parity] = totals[parity]
                 else:
                     added[parity] += totals[parity]
-        if first:
-            for p in range(pieces + AHEAD, pieces + GROUP * GROUPS_AHEAD):
-                start_piece(p)
         for parity in range(2):
             for k in range(TAPS):
                 for tile in range(tiles):
@@ -148,28 +142,29 @@
                     slab = added[parity, pl.ds(TAPS * kept + k // SUBLANES * SUBLANES, SUBLANES), lanes]
                     middle[parity, k % 2, to] += jnp.where(sublane == k % SUBLANES, slab, 0.0)
 
-    group_step(0, True)
+    for g in range(BY_PIECE):
+        group_step(g, True, g == 0)
+    for step in range(BY_PIECE * pieces + AHEAD, BY_PIECE * pieces + frames - BY_PIECE * GROUP):
+        start(step)
 
     def later_step(g, carry):
         group_step(g, False)
         return carry
 
-    lax.fori_loop(1, groups, later_step, 0)
+    lax.fori_loop(BY_PIECE, groups, later_step, 0)
 
     low = lax.broadcasted_iota(jnp.int32, (1, LANES), 1) < LANES // 2
 
-    def joined(ref, parity, tile):
-        later = pltpu.roll(ref[parity, 1, tile], LANES // 2, 1)
-        if tile == 0:
-            earlier = jnp.zeros_like(later)
-        else:
-            earlier = pltpu.roll(ref[parity, 1, tile - 1], LANES // 2, 1)
-        return ref[parity, 0, tile] + jnp.where(low, earlier, later)
+    def joined(ref, parity):
+        earlier = None
+        for tile in range(ref.shape[2]):
+            later = pltpu.roll(ref[parity, 1, tile], LANES // 2, 1)
+            yield ref[parity, 0, tile] + jnp.where(low, 0.0 if earlier is None else earlier, later)
+            earlier = later
 
     block = 2 * 2 * half_rows
-    for tile in range(sums.shape[2]):
-        e = joined(sums, 0, tile)
-        o = joined(sums, 1, tile)
+    both = [joined(sums, 0), joined(sums, 1), joined(middle, 0), joined(middle, 1)]
+    for tile, (e, o, e_mid, o_mid) in enumerate(zip(*both)):
         e_re, e_im, o_re, o_im = e[:half], e[half:], o[:half], o[half:]
         real = pl.ds(tile, half, stride=block)
         imag = pl.ds(2 * half_rows + tile, half, stride=block)
@@ -177,10 +172,8 @@
         plus[imag, :] = e_im - o_re
         minus[real, :] = e_re - o_im
         minus[imag, :] = -e_im - o_re
-        centre[tile : tile + 1, :] = jnp.sum(joined(middle, 0, tile), axis=0, keepdims=True)
-        centre[2 * half_rows + tile : 2 * half_rows + tile + 1, :] = -jnp.sum(
-            joined(middle, 1, tile), axis=0, keepdims=True
-        )
+        centre[tile : tile + 1, :] = jnp.sum(e_mid, axis=0, keepdims=True)
+        centre[2 * half_rows + tile : 2 * half_rows + tile + 1, :] = -jnp.sum(o_mid, axis=0, keepdims=True)
     for h in range(1, half + 1):
         rows = slice((h - 1) * block, h * block)
         out[half - h] = minus[rows].astype(jnp.bfloat16)
@@ -213,7 +206,7 @@
             pltpu.VMEM((half * 4 * half_rows, LANES), jnp.float32),
             pltpu.VMEM((half * 4 * half_rows, LANES), jnp.float32),
             pltpu.VMEM((4 * half_rows, LANES), jnp.float32),
-            pltpu.SemaphoreType.DMA((FRAME // 2 // DEPTH, GROUP + 1)),
+            pltpu.SemaphoreType.DMA((BY_PIECE * len(PIECES), GROUP + 1)),
             pltpu.SemaphoreType.DMA((frames,)),
         ],
         compiler_params=pltpu.CompilerParams(vmem_limit_bytes=(52 if rows <= 512 else 63) << 20),

time: 30.4 us -> 30.2 us (level)
  no operation moved by 1% of the time
where the time goes in v4:
time: 30.2 us; the launch traced here: 30.1 us
  blocking collectives  17.3 us (57%)
  Pallas kernels  12.8 us (42%)
    all_to_all x1, blocking collectives, on_device(): lax.all_to_all(partial, ('stn', 'tm'), split_axis=0, concat_axis=0, tiled...  17.3 us
    pallas_call x1, Pallas kernels, block_spectra(): pl.pallas_call(functools.partial(spectra_kernel, kept, frames, inputs), o...  11.1 us
    pallas_call x1, Pallas kernels, correlate(): pl.pallas_call(functools.partial(correlate_kernel, stations, time_blocks,...  1.7 us

profile of v4, /device:TPU:0, one launch (start us, length us, event | category | flops | bytes accessed | tf_op | source)
XLA Modules:
  0.0 30.1 jit_solution(3795039851741806121)
XLA Ops:
  0.0 11.1 %shard_map.28 = bf16[32,32,128]{2,1,0:T(8,128)(2,1)S(1)} custom-call(bf16[64,131072]{1,0:T(8,128)(2,1)} %samples.1, f32[2,56,4096]{2,1,0:T(8,128)} %constant.2.clone.table), custom_call_target="tpu_custom_call" | custom-call | tf_op jit(solution)/shard_map/pallas_call | solution.py:194
  11.1 17.3 %all_to_all.5.arrived = bf16[32,32,128]{2,1,0:T(8,128)(2,1)S(1)} all-to-all(bf16[32,32,128]{2,1,0:T(8,128)(2,1)S(1)} %shard_map.28), channel_id=1, replica_groups=mesh['stn'=8,'tm'=4] {'stn','tm'}, dimensions={0} | all-to-all | bytes 524288 | tf_op jit(solution)/shard_map/all_to_all | solution.py:291
  28.4 1.7 %shard_map.29 = f32[1,2,512,512]{3,2,1,0:T(8,128)} custom-call(bf16[32,32,128]{2,1,0:T(8,128)(2,1)S(1)} %all_to_all.5.arrived), custom_call_target="tpu_custom_call" | custom-call | tf_op jit(solution)/shard_map/pallas_call | solution.py:272

commit v5 on v4

--- a/solution.py
+++ b/solution.py
@@ -46,8 +46,8 @@
     return np.stack(stacks).astype(np.float32)
 
 
-def spectra_kernel(kept, frames, inputs, samples, table, out, held, table_v, weights, added, sums, middle, plus,
-                   minus, centre, piece_sem, frame_sem):
+def spectra_kernel(kept, frames, inputs, samples, table, out, held, table_v, weights, added, sums, middle, centre,
+                   piece_sem, frame_sem):
     half = kept // 2
     groups = frames // GROUP
     columns = GROUP * inputs
@@ -81,7 +81,7 @@
 
     for step in range(AHEAD):
         start(step)
-    for ref in (sums, middle, plus, minus, centre):
+    for ref in (sums, middle, centre):
         ref[...] = jnp.zeros_like(ref)
 
     even_lane = lax.broadcasted_iota(jnp.int32, (inputs, LANES), 1) % 2 == 0
@@ -162,30 +162,31 @@
             yield ref[parity, 0, tile] + jnp.where(low, 0.0 if earlier is None else earlier, later)
             earlier = later
 
-    block = 2 * 2 * half_rows
+    rows = {name: [] for name in range(4)}
     both = [joined(sums, 0), joined(sums, 1), joined(middle, 0), joined(middle, 1)]
     for tile, (e, o, e_mid, o_mid) in enumerate(zip(*both)):
         e_re, e_im, o_re, o_im = e[:half], e[half:], o[:half], o[half:]
-        real = pl.ds(tile, half, stride=block)
-        imag = pl.ds(2 * half_rows + tile, half, stride=block)
-        plus[real, :] = e_re + o_im
-        plus[imag, :] = e_im - o_re
-        minus[real, :] = e_re - o_im
-        minus[imag, :] = -e_im - o_re
+        for name, value in enumerate((e_re + o_im, e_im - o_re, e_re - o_im, -e_im - o_re)):
+            rows[name].append(value)
         centre[tile : tile + 1, :] = jnp.sum(e_mid, axis=0, keepdims=True)
         centre[2 * half_rows + tile : 2 * half_rows + tile + 1, :] = -jnp.sum(o_mid, axis=0, keepdims=True)
-    for h in range(1, half + 1):
-        rows = slice((h - 1) * block, h * block)
-        out[half - h] = minus[rows].astype(jnp.bfloat16)
-        if h < half:
-            out[half + h] = plus[rows].astype(jnp.bfloat16)
+    for name in range(4):
+        values = rows[name] + [jnp.zeros((half, LANES), jnp.float32)] * (2 * half_rows - len(rows[name]))
+        part = pl.ds(2 * half_rows * (name % 2), 2 * half_rows)
+        for first in range(0, half, SUBLANES):
+            turned = jnp.swapaxes(jnp.stack([v[first : first + SUBLANES] for v in values]), 0, 1).astype(jnp.bfloat16)
+            for i in range(SUBLANES):
+                h = first + i + 1
+                if name >= 2:
+                    out[half - h, part] = turned[i]
+                elif h < half:
+                    out[half + h, part] = turned[i]
     out[half] = centre[...].astype(jnp.bfloat16)
 
 
 def block_spectra(samples, kept):
     inputs, count = samples.shape
     frames = count // FRAME
-    half = kept // 2
     half_rows = frames * inputs // LANES
     table = tables(kept)
     rows = TAPS * kept + 2 * SUBLANES
@@ -203,8 +204,6 @@
             pltpu.VMEM((2, rows, GROUP * inputs), jnp.float32),
             pltpu.VMEM((2, 2, tiles, kept, LANES), jnp.float32),
             pltpu.VMEM((2, 2, tiles, SUBLANES, LANES), jnp.float32),
-            pltpu.VMEM((half * 4 * half_rows, LANES), jnp.float32),
-            pltpu.VMEM((half * 4 * half_rows, LANES), jnp.float32),
             pltpu.VMEM((4 * half_rows, LANES), jnp.float32),
             pltpu.SemaphoreType.DMA((BY_PIECE * len(PIECES), GROUP + 1)),
             pltpu.SemaphoreType.DMA((frames,)),

time: 30.2 us -> 30 us (level)
  no operation moved by 1% of the time
where the time goes in v5:
time: 30 us; the launch traced here: 29.8 us
  blocking collectives  17.3 us (58%)
  Pallas kernels  12.5 us (42%)
    all_to_all x1, blocking collectives, on_device(): lax.all_to_all(partial, ('stn', 'tm'), split_axis=0, concat_axis=0, tiled...  17.3 us
    pallas_call x1, Pallas kernels, block_spectra(): pl.pallas_call(functools.partial(spectra_kernel, kept, frames, inputs), o...  10.8 us
    pallas_call x1, Pallas kernels, correlate(): pl.pallas_call(functools.partial(correlate_kernel, stations, time_blocks,...  1.7 us

profile of v5, /device:TPU:0, one launch (start us, length us, event | category | flops | bytes accessed | tf_op | source)
XLA Modules:
  0.0 29.8 jit_solution(26032039613722882)
XLA Ops:
  0.0 10.8 %shard_map.28 = bf16[32,32,128]{2,1,0:T(8,128)(2,1)S(1)} custom-call(bf16[64,131072]{1,0:T(8,128)(2,1)} %samples.1, f32[2,56,4096]{2,1,0:T(8,128)} %constant.2.clone.table), custom_call_target="tpu_custom_call" | custom-call | tf_op jit(solution)/shard_map/pallas_call | solution.py:195
  10.8 17.3 %all_to_all.5.arrived = bf16[32,32,128]{2,1,0:T(8,128)(2,1)S(1)} all-to-all(bf16[32,32,128]{2,1,0:T(8,128)(2,1)S(1)} %shard_map.28), channel_id=1, replica_groups=mesh['stn'=8,'tm'=4] {'stn','tm'}, dimensions={0} | all-to-all | bytes 524288 | tf_op jit(solution)/shard_map/all_to_all | solution.py:290
  28.1 1.7 %shard_map.29 = f32[1,2,512,512]{3,2,1,0:T(8,128)} custom-call(bf16[32,32,128]{2,1,0:T(8,128)(2,1)S(1)} %all_to_all.5.arrived), custom_call_target="tpu_custom_call" | custom-call | tf_op jit(solution)/shard_map/pallas_call | solution.py:271
